TPU v7x, 32 devices: a whole 2x2x4 slice. The times are simulated.
32 devices in a mesh: img: 2 (over x), row: 4 (over z), col: 4 (over y, core).
Axes of the slice: x: 2, y: 2, z: 4, core: 2. Of those that a mesh axis runs over, the one named last changes fastest.
Arguments:
- latent: bfloat16 [128, 64, 1280], P(('img', 'row'), 'col'), parts along dimension 0, may hold values from -240 to 240
- norm_gain: float32 [1280], replicated, may hold values from 0.1 to 1.9
- norm_shift: float32 [1280], replicated, may hold values from -3 to 3
- query_weight: bfloat16 [1280, 768], replicated, may hold values from -0.25 to 0.25
- key_weight: bfloat16 [1280, 768], replicated, may hold values from -0.25 to 0.25
- value_weight: bfloat16 [1280, 768], replicated, may hold values from -0.15625 to 0.15625
- output_weight: bfloat16 [768, 1280], replicated, may hold values from -0.875 to 0.875
- output_bias: float32 [1280], replicated, may hold values from -3 to 3
Outputs:
- attended: bfloat16 [128, 64, 1280], P(('img', 'row'), 'col'), parts along dimension 0
There are 2 independent parts, one for each index of `img`. A program takes and returns all parts, laid end to end along the dimension named above; an argument that names none is the same for every part. Nothing has to cross between parts.
All inputs are finite; a program needn't handle non-finite values.
Results may differ from a plain program's by a relative error of at most 0.012.
The roundings to bfloat16 on the way count: a program that leaves them out, or rounds other values in their place, can miss the bound.
Values may be sent and summed in bfloat16 or wider, within the bound.
A program may use at most 128 MiB of HBM per device.

v0:
```python
import math
import jax
import jax.numpy as jnp
from jax import lax
from jax.sharding import PartitionSpec as P

GROUPS = 32
HD = 64


def attend(carry, piece, queries):
    keys, values = piece
    heads_here = queries.shape[1] // HD
    scale = 1.0 / math.sqrt(HD)
    query_heads = queries.reshape(queries.shape[0], heads_here, HD).transpose(1, 0, 2)
    key_heads = keys.reshape(keys.shape[0], heads_here, HD).transpose(1, 0, 2)
    value_heads = values.reshape(values.shape[0], heads_here, HD).transpose(1, 0, 2)

    def per_head(items):
        query_one, key_one, value_one, peak_old, total_old, mixed_old = items
        scores = jnp.dot(query_one, key_one.T, preferred_element_type=jnp.float32) * scale
        peak_new = jnp.maximum(peak_old, jnp.max(scores, axis=1))
        factor = jnp.exp(peak_old - peak_new)
        weights = jnp.exp(scores - peak_new[:, None])
        total_new = total_old * factor + jnp.sum(weights, axis=1)
        rounded = weights.astype(jnp.bfloat16)
        mixed_new = mixed_old * factor[:, None] + jnp.dot(
            rounded, value_one, preferred_element_type=jnp.float32
        )
        return (peak_new, total_new, mixed_new)

    return lax.map(per_head, (query_heads, key_heads, value_heads) + tuple(carry))


def start_state(queries):
    heads_here = queries.shape[1] // HD
    count = queries.shape[0]
    peak = jnp.full((heads_here, count), -1e30, jnp.float32)
    total = jnp.zeros((heads_here, count), jnp.float32)
    mixed = jnp.zeros((heads_here, count, HD), jnp.float32)
    return (peak, total, mixed)


def finish(state):
    peak, total, mixed = state
    heads_here, count, _ = mixed.shape
    result = mixed / total[:, :, None]
    return result.transpose(1, 0, 2).reshape(count, heads_here * HD).astype(jnp.bfloat16)


def local(
    latent,
    norm_gain,
    norm_shift,
    query_weight,
    key_weight,
    value_weight,
    output_weight,
    output_bias,
):
    rows_here, cols_here, width = latent.shape
    tok_count = rows_here * cols_here
    wide = latent.reshape(tok_count, width).astype(jnp.float32)
    grouped = wide.reshape(tok_count, GROUPS, width // GROUPS)
    entries = float(tok_count * lax.axis_size("row") * lax.axis_size("col") * (width // GROUPS))
    group_total = lax.psum(jnp.sum(grouped, axis=(0, 2)), ("row", "col"))
    mean = group_total / entries
    centered = grouped - mean[None, :, None]
    spread = lax.psum(jnp.sum(centered * centered, axis=(0, 2)), ("row", "col"))
    variance = spread / entries
    scaled = (centered * lax.rsqrt(variance + 1e-05)[None, :, None]).reshape(tok_count, width)
    normed = (scaled * norm_gain + norm_shift).astype(jnp.bfloat16)
    queries = jnp.dot(normed, query_weight, preferred_element_type=jnp.float32).astype(jnp.bfloat16)
    keys = jnp.dot(normed, key_weight, preferred_element_type=jnp.float32).astype(jnp.bfloat16)
    values = jnp.dot(normed, value_weight, preferred_element_type=jnp.float32).astype(jnp.bfloat16)
    state = attend(
        start_state(queries),
        (
            lax.all_gather(keys, ("row", "col"), axis=0, tiled=True),
            lax.all_gather(values, ("row", "col"), axis=0, tiled=True),
        ),
        queries,
    )
    mixed = finish(state)
    result = jnp.dot(mixed, output_weight, preferred_element_type=jnp.float32) + output_bias
    return result.astype(jnp.bfloat16).reshape(rows_here, cols_here, width)


def solution(mesh):
    placed = (P(("img", "row"), "col", None), P(), P(), P(), P(), P(), P(), P())
    return jax.shard_map(
        local, mesh=mesh, in_specs=placed, out_specs=P(("img", "row"), "col", None), check_vma=False
    )
```

profile of v0, /device:TPU:0, one launch (start us, length us, event | category | flops | bytes accessed | tf_op | source)
XLA Modules:
  0.0 272.7 jit_solution(14949438277409626070)
XLA Ops:
  6.5 1.3 convert_reduce_fusion
  7.9 0.1 reduce_sum.36
  8.0 0.1 reduce_sum.37
  8.1 34.9 %psum.14 = f32[32]{0:T(128)S(1)} all-reduce(f32[32]{0:T(128)S(1)} %reduce_sum.37), channel_id=1, replica_groups=mesh['img'=2,'row'=4,'col'=4] {'row','col'}, use_global_device_ids=true, to_apply=%region_2.0 | all-reduce | flops 32 | bytes 256 | tf_op jit(solution)/shard_map/psum | solution.py:66
  43.0 0.1 sub.41
  43.1 0.1 sub.42
  43.2 1.3 multiply_reduce_fusion
  44.5 0.1 reduce_sum.47
  44.5 0.1 reduce_sum.48
  44.7 29.5 %psum.15 = f32[32]{0:T(128)S(1)} all-reduce(f32[32]{0:T(128)S(1)} %reduce_sum.48), channel_id=1, replica_groups=mesh['img'=2,'row'=4,'col'=4] {'row','col'}, use_global_device_ids=true, to_apply=%region_5.6 | all-reduce | flops 32 | bytes 256 | tf_op jit(solution)/shard_map/psum | solution.py:69
  74.2 0.1 mul.49
  74.2 0.1 mul.50
  74.3 1.3 fusion.27
  75.7 0.0 copy-start.1
  75.7 3.2 %convolution_convert_fusion = bf16[256,768]{1,0:T(8,128)(2,1)} fusion(bf16[256,1280]{1,0:T(8,128)(2,1)S(1)} %fusion.27, bf16[1280,768]{1,0:T(8,128)(2,1)} %param.15), kind=kOutput, calls=%fused_computation.28 | convolution fusion | flops 503513088 | bytes 3014656 | tf_op jit(solution)/shard_map/dot_general | solution.py:75
  78.9 0.0 all-gather.5.cloned.1.call-update
  78.9 0.0 all-gather.3.cloned.1.call-start
  79.0 3.0 %convolution_convert_fusion.1 = bf16[256,768]{1,0:T(8,128)(2,1)} fusion(bf16[256,1280]{1,0:T(8,128)(2,1)S(1)} %fusion.27, bf16[1280,768]{1,0:T(8,128)(2,1)} %param.14), kind=kOutput, calls=%fused_computation.29 | convolution fusion | flops 503513088 | bytes 3014656 | tf_op jit(solution)/shard_map/dot_general | solution.py:74
  81.9 0.0 all-gather.3.cloned.1.call-update
  82.0 2.5 convolution_convert_fusion.2
  84.5 0.2 copy.18
  84.7 53.5 %all-gather.5.cloned.1.call-done = bf16[4096,768]{1,0:T(8,128)(2,1)} async-done(((bf16[256,768]{1,0:T(8,128)(2,1)}), bf16[4096,768]{1,0:T(8,128)(2,1)}) %all-gather.5.cloned.1.call-update) | async-done | bytes 6291472 | tf_op jit(solution)/shard_map/all_gather | solution.py:80
  138.2 8.8 %copy.20 = bf16[4096,768]{0,1:T(8,128)(2,1)} copy(bf16[4096,768]{1,0:T(8,128)(2,1)} %all-gather.5.cloned.1.call-done) | data formatting | bytes 12582912 | tf_op jit(solution)/shard_map/all_gather | solution.py:80
  146.9 54.0 %all-gather.3.cloned.1.call-done = bf16[4096,768]{1,0:T(8,128)(2,1)} async-done(((bf16[256,768]{1,0:T(8,128)(2,1)}), bf16[4096,768]{1,0:T(8,128)(2,1)}) %all-gather.3.cloned.1.call-update) | async-done | bytes 6291472 | tf_op jit(solution)/shard_map/all_gather | solution.py:79
  200.9 8.6 %copy.19 = bf16[4096,768]{0,1:T(8,128)(2,1)} copy(bf16[4096,768]{1,0:T(8,128)(2,1)} %all-gather.3.cloned.1.call-done) | data formatting | bytes 12582912 | tf_op jit(solution)/shard_map/all_gather | solution.py:79
  209.6 54.7 %while.12 = (s32[]{:T(128)}, f32[12,256]{1,0:T(8,128)S(1)}, f32[12,256,64]{1,2,0:T(8,128)S(1)}, bf16[12,256,64]{1,2,0:T(8,128)(2,1)S(1)}, bf16[12,4096,64]{1,2,0...) while((s32[]{:T(128)}, f32[12,256]{1,0:T(8,128)S(1)}, ...), condition=%wide.region_9.10_spmd, body=%wide.region_6.9_spmd.sunk | while | flops 274744064 | bytes 13745249 | solution.py:32
  209.6 1.9 fusion.44
  211.4 0.7 fusion.45
  212.2 1.9 fusion.46
  214.1 1.9 fusion.44
  216.0 0.7 fusion.45
  216.7 1.9 fusion.46
  218.7 1.9 fusion.44
  220.5 0.7 fusion.45
  221.3 1.9 fusion.46
  223.2 1.9 fusion.44
  225.1 0.7 fusion.45
  225.8 1.9 fusion.46
  227.8 1.9 fusion.44
  229.6 0.7 fusion.45
  230.4 1.9 fusion.46
  232.3 1.9 fusion.44
  234.2 0.7 fusion.45
  234.9 1.9 fusion.46
  236.9 1.9 fusion.44
  238.8 0.7 fusion.45
  239.5 1.9 fusion.46
  241.5 1.9 fusion.44
  243.3 0.7 fusion.45
  244.0 1.9 fusion.46
  246.0 1.9 fusion.44
  247.9 0.7 fusion.45
  248.6 1.9 fusion.46
  250.6 1.9 fusion.44
  252.4 0.7 fusion.45
  253.2 1.9 fusion.46
  255.1 1.9 fusion.44
  257.0 0.7 fusion.45
  257.7 1.9 fusion.46
  259.7 1.9 fusion.44
  261.5 0.7 fusion.45
  262.3 1.9 fusion.46
  264.2 0.1 divide_convert_fusion
  264.3 1.5 fusion.23
  (46 shorter events, 0.7 us)
Async XLA Ops:
  6.5 257.8 %copy-start = (bf16[768,1280]{1,0:T(8,128)(2,1)S(1)}, bf16[768,1280]{1,0:T(8,128)(2,1)}, u32[]{:S(2)}) copy-start(bf16[768,1280]{1,0:T(8,128)(2,1)} %param.16) | copy-start | bytes 5898244
  6.5 131.6 %all-gather.5.cloned.1.call-start = ((), (), s32[]{:S(2)}) async-start(), calls=%async_computation.1 | async-start | bytes 6684672 | tf_op jit(solution)/shard_map/all_gather | solution.py:80
  75.7 6.3 %copy-start.1 = (bf16[256,1280]{1,0:T(8,128)(2,1)}, bf16[256,1280]{1,0:T(8,128)(2,1)S(1)}, u32[]{:S(2)}) copy-start(bf16[256,1280]{1,0:T(8,128)(2,1)S(1)} %fusion.27) | copy-start | bytes 1966084
  78.9 122.0 %all-gather.3.cloned.1.call-start = ((), (), s32[]{:S(2)}) async-start(), calls=%async_computation | async-start | bytes 6684672 | tf_op jit(solution)/shard_map/all_gather | solution.py:79
  209.6 54.8 %copy-start.2 = (f32[1280]{0:T(1024)S(1)}, f32[1280]{0:T(1024)}, u32[]{:S(2)}) copy-start(f32[1280]{0:T(1024)} %param.17) | copy-start | bytes 15364
Sparse Core Ops, SparseCore 0:
  79.0 59.0 all-gather.4
  140.5 60.4 all-gather.2
where the time goes:
time: 275 us; the launch traced here: 273 us
  waiting for transfers between devices  108 us (39%)
  blocking collectives  64.4 us (23%)
  matrix products  55.3 us (20%)
  local copies, waits for them, and re-layouts  18.5 us (7%)
  between operations  13.5 us (5%)
  other arithmetic  13.1 us (5%)
    all_gather x1, waiting for transfers between devices, local(): lax.all_gather(keys, ('row', 'col'), axis=0, tiled=True)  54 us
    all_gather x1, waiting for transfers between devices, local(): lax.all_gather(values, ('row', 'col'), axis=0, tiled=True)  53.5 us
    psum x1, blocking collectives, local(): group_total = lax.psum(jnp.sum(grouped, axis=(0, 2)), ('row', 'col'))  34.9 us
    psum x1, blocking collectives, local(): spread = lax.psum(jnp.sum(centered * centered, axis=(0, 2)), ('row', 'col'))  29.5 us
    dot_general x12, matrix products, per_head(): jnp.dot(rounded, value_one, preferred_element_type=jnp.float32)  22.8 us
    dot_general x12, matrix products, per_head(): jnp.dot(query_one, key_one.T, preferred_element_type=jnp.float32) * scale  22.3 us
    all_gather x1, local copies, waits for them, and re-layouts, local(): lax.all_gather(values, ('row', 'col'), axis=0, tiled=True)  8.75 us
    all_gather x1, local copies, waits for them, and re-layouts, local(): lax.all_gather(keys, ('row', 'col'), axis=0, tiled=True)  8.61 us
  transfers between devices with their start and end apart: 2, of which 2 were waited for; matrix products, arithmetic and copies ran while one was open for 5% of the time, Pallas kernels for 0%

commit v1 on v0

--- a/solution.py
+++ b/solution.py
@@ -63,7 +63,7 @@
     wide = latent.reshape(tok_count, width).astype(jnp.float32)
     grouped = wide.reshape(tok_count, GROUPS, width // GROUPS)
     entries = float(tok_count * lax.axis_size("row") * lax.axis_size("col") * (width // GROUPS))
-    group_total = lax.psum(jnp.sum(grouped, axis=(0, 2)), ("row", "col"))
+    group_total = lax.psum(lax.psum(jnp.sum(grouped, axis=(0, 2)), "col"), "row")
     mean = group_total / entries
     centered = grouped - mean[None, :, None]
     spread = lax.psum(jnp.sum(centered * centered, axis=(0, 2)), ("row", "col"))

time: 275 us -> 260 us (0.945)
  blocking collectives: 64.4 us -> 49.8 us
    psum x1 -> x2, blocking collectives: 34.9 us -> 20.3 us  [the longest x1 11.9 us: local(): lax.psum(lax.psum(jnp.sum(grouped, axis=(0, 2)), 'col'), 'row')]
  transfers between devices with their start and end apart: 2 -> 2, of which waited for: 2 -> 2; matrix products, arithmetic and copies ran while one was open for 5% -> 6% of each run, Pallas kernels for 0% -> 0%
where the time goes in v1:
time: 260 us; the launch traced here: 258 us
  waiting for transfers between devices  108 us (42%)
  matrix products  55.3 us (21%)
  blocking collectives  49.8 us (19%)
  local copies, waits for them, and re-layouts  18.5 us (7%)
  between operations  13.5 us (5%)
  other arithmetic  13.1 us (5%)
    all_gather x1, waiting for transfers between devices, local(): lax.all_gather(keys, ('row', 'col'), axis=0, tiled=True)  54 us
    all_gather x1, waiting for transfers between devices, local(): lax.all_gather(values, ('row', 'col'), axis=0, tiled=True)  53.5 us
    psum x1, blocking collectives, local(): spread = lax.psum(jnp.sum(centered * centered, axis=(0, 2)), ('row', 'col'))  29.5 us
    dot_general x12, matrix products, per_head(): jnp.dot(rounded, value_one, preferred_element_type=jnp.float32)  22.8 us
    dot_general x12, matrix products, per_head(): jnp.dot(query_one, key_one.T, preferred_element_type=jnp.float32) * scale  22.3 us
    psum x1, blocking collectives, local(): lax.psum(lax.psum(jnp.sum(grouped, axis=(0, 2)), 'col'), 'row')  11.9 us
    all_gather x1, local copies, waits for them, and re-layouts, local(): lax.all_gather(values, ('row', 'col'), axis=0, tiled=True)  8.75 us
    all_gather x1, local copies, waits for them, and re-layouts, local(): lax.all_gather(keys, ('row', 'col'), axis=0, tiled=True)  8.61 us
  transfers between devices with their start and end apart: 2, of which 2 were waited for; matrix products, arithmetic and copies ran while one was open for 6% of the time, Pallas kernels for 0%

profile of v1, /device:TPU:0, one launch (start us, length us, event | category | flops | bytes accessed | tf_op | source)
XLA Modules:
  0.0 258.1 jit_solution(5565774108331651904)
XLA Ops:
  6.5 1.3 convert_reduce_fusion
  7.9 0.1 reduce_sum.36
  8.0 0.1 reduce_sum.37
  8.1 8.4 %psum.21 = f32[32]{0:T(128)S(1)} all-reduce(f32[32]{0:T(128)S(1)} %reduce_sum.37), channel_id=1, replica_groups=mesh['img'=2,'row'=4,'col'=4] {'col'}, use_global_device_ids=true, to_apply=%region_2.0 | all-reduce | flops 32 | bytes 256 | tf_op jit(solution)/shard_map/psum | solution.py:66
  16.4 11.9 %psum.22 = f32[32]{0:T(128)S(1)} all-reduce(f32[32]{0:T(128)S(1)} %psum.21), channel_id=1, replica_groups=mesh['img'=2,'row'=4,'col'=4] {'row'}, use_global_device_ids=true, to_apply=%region_3.0 | all-reduce | flops 32 | bytes 256 | tf_op jit(solution)/shard_map/psum | solution.py:66
  28.4 0.1 sub.41
  28.5 0.1 sub.42
  28.6 1.3 multiply_reduce_fusion
  29.8 0.1 reduce_sum.47
  29.9 0.1 reduce_sum.48
  30.1 29.5 %psum.23 = f32[32]{0:T(128)S(1)} all-reduce(f32[32]{0:T(128)S(1)} %reduce_sum.48), channel_id=1, replica_groups=mesh['img'=2,'row'=4,'col'=4] {'row','col'}, use_global_device_ids=true, to_apply=%region_6.7 | all-reduce | flops 32 | bytes 256 | tf_op jit(solution)/shard_map/psum | solution.py:69
  59.6 0.1 mul.49
  59.6 0.1 mul.50
  59.7 1.3 fusion.27
  61.1 3.2 %convolution_convert_fusion = bf16[256,768]{1,0:T(8,128)(2,1)} fusion(bf16[256,1280]{1,0:T(8,128)(2,1)S(1)} %fusion.27, bf16[1280,768]{1,0:T(8,128)(2,1)} %param.15), kind=kOutput, calls=%fused_computation.28 | convolution fusion | flops 503513088 | bytes 3014656 | tf_op jit(solution)/shard_map/dot_general | solution.py:75
  64.3 0.0 all-gather.5.cloned.1.call-update
  64.3 0.0 all-gather.3.cloned.1.call-start
  64.4 3.0 %convolution_convert_fusion.1 = bf16[256,768]{1,0:T(8,128)(2,1)} fusion(bf16[256,1280]{1,0:T(8,128)(2,1)S(1)} %fusion.27, bf16[1280,768]{1,0:T(8,128)(2,1)} %param.14), kind=kOutput, calls=%fused_computation.29 | convolution fusion | flops 503513088 | bytes 3014656 | tf_op jit(solution)/shard_map/dot_general | solution.py:74
  67.3 0.0 all-gather.3.cloned.1.call-update
  67.4 2.5 convolution_convert_fusion.2
  69.9 0.2 copy.18
  70.1 53.5 %all-gather.5.cloned.1.call-done = bf16[4096,768]{1,0:T(8,128)(2,1)} async-done(((bf16[256,768]{1,0:T(8,128)(2,1)}), bf16[4096,768]{1,0:T(8,128)(2,1)}) %all-gather.5.cloned.1.call-update) | async-done | bytes 6291472 | tf_op jit(solution)/shard_map/all_gather | solution.py:80
  123.6 8.8 %copy.20 = bf16[4096,768]{0,1:T(8,128)(2,1)} copy(bf16[4096,768]{1,0:T(8,128)(2,1)} %all-gather.5.cloned.1.call-done) | data formatting | bytes 12582912 | tf_op jit(solution)/shard_map/all_gather | solution.py:80
  132.3 54.0 %all-gather.3.cloned.1.call-done = bf16[4096,768]{1,0:T(8,128)(2,1)} async-done(((bf16[256,768]{1,0:T(8,128)(2,1)}), bf16[4096,768]{1,0:T(8,128)(2,1)}) %all-gather.3.cloned.1.call-update) | async-done | bytes 6291472 | tf_op jit(solution)/shard_map/all_gather | solution.py:79
  186.3 8.6 %copy.19 = bf16[4096,768]{0,1:T(8,128)(2,1)} copy(bf16[4096,768]{1,0:T(8,128)(2,1)} %all-gather.3.cloned.1.call-done) | data formatting | bytes 12582912 | tf_op jit(solution)/shard_map/all_gather | solution.py:79
  194.9 54.7 %while.12 = (s32[]{:T(128)}, f32[12,256]{1,0:T(8,128)S(1)}, f32[12,256,64]{1,2,0:T(8,128)S(1)}, bf16[12,256,64]{1,2,0:T(8,128)(2,1)S(1)}, bf16[12,4096,64]{1,2,0...) while((s32[]{:T(128)}, f32[12,256]{1,0:T(8,128)S(1)}, ...), condition=%wide.region_10.11_spmd, body=%wide.region_7.10_spmd.sunk | while | flops 274744064 | bytes 13745249 | solution.py:32
  194.9 1.9 fusion.44
  196.8 0.7 fusion.45
  197.6 1.9 fusion.46
  199.5 1.9 fusion.44
  201.4 0.7 fusion.45
  202.1 1.9 fusion.46
  204.1 1.9 fusion.44
  205.9 0.7 fusion.45
  206.7 1.9 fusion.46
  208.6 1.9 fusion.44
  210.5 0.7 fusion.45
  211.2 1.9 fusion.46
  213.2 1.9 fusion.44
  215.1 0.7 fusion.45
  215.8 1.9 fusion.46
  217.7 1.9 fusion.44
  219.6 0.7 fusion.45
  220.3 1.9 fusion.46
  222.3 1.9 fusion.44
  224.2 0.7 fusion.45
  224.9 1.9 fusion.46
  226.8 1.9 fusion.44
  228.7 0.7 fusion.45
  229.4 1.9 fusion.46
  231.4 1.9 fusion.44
  233.3 0.7 fusion.45
  234.0 1.9 fusion.46
  236.0 1.9 fusion.44
  237.8 0.7 fusion.45
  238.6 1.9 fusion.46
  240.5 1.9 fusion.44
  242.4 0.7 fusion.45
  243.1 1.9 fusion.46
  245.1 1.9 fusion.44
  246.9 0.7 fusion.45
  247.7 1.9 fusion.46
  249.6 0.1 divide_convert_fusion
  249.7 1.6 fusion.23
  (47 shorter events, 0.8 us)
Async XLA Ops:
  6.5 243.2 %copy-start = (bf16[768,1280]{1,0:T(8,128)(2,1)S(1)}, bf16[768,1280]{1,0:T(8,128)(2,1)}, u32[]{:S(2)}) copy-start(bf16[768,1280]{1,0:T(8,128)(2,1)} %param.16) | copy-start | bytes 5898244
  6.5 117.0 %all-gather.5.cloned.1.call-start = ((), (), s32[]{:S(2)}) async-start(), calls=%async_computation.1 | async-start | bytes 6684672 | tf_op jit(solution)/shard_map/all_gather | solution.py:80
  61.1 6.3 %copy-start.1 = (bf16[256,1280]{1,0:T(8,128)(2,1)}, bf16[256,1280]{1,0:T(8,128)(2,1)S(1)}, u32[]{:S(2)}) copy-start(bf16[256,1280]{1,0:T(8,128)(2,1)S(1)} %fusion.27) | copy-start | bytes 1966084
  64.3 122.0 %all-gather.3.cloned.1.call-start = ((), (), s32[]{:S(2)}) async-start(), calls=%async_computation | async-start | bytes 6684672 | tf_op jit(solution)/shard_map/all_gather | solution.py:79
  194.9 54.8 %copy-start.2 = (f32[1280]{0:T(1024)S(1)}, f32[1280]{0:T(1024)}, u32[]{:S(2)}) copy-start(f32[1280]{0:T(1024)} %param.17) | copy-start | bytes 15364
Sparse Core Ops, SparseCore 0:
  64.4 59.0 all-gather.4
  125.9 60.4 all-gather.2
